TPU v7x, 256 devices: a whole 4x4x8 slice. The times are simulated.
256 devices in a mesh: row: 16 (over x_hi, y, core), col: 16 (over z, x_lo).
Axes of the slice: x: 4 (x_hi: 2, x_lo: 2; x = x_hi * 2 + x_lo), y: 4, z: 8, core: 2. Of those that a mesh axis runs over, the one named last changes fastest.
Arguments:
- basis: float32 [4096, 6144], P('row', 'col'), may hold values from -0.625 to 0.625
- image: float32 [4096, 6144], P('row', 'col'), may hold values from -0.625 to 0.625
- coeffs: float32 [6144, 4096], P('row', 'col'), may hold values from -6 to 6
Outputs:
- gram: float32 [6144, 6144], P('row', 'col')
- stiffness: float32 [6144, 6144], P('row', 'col')
- rotated: float32 [4096, 4096], P('row', 'col')
All inputs are finite; a program needn't handle non-finite values.
Results may differ from a plain program's by a relative error of at most 0.00007.
Values sent between devices are 32-bit elements; how exact they have to be, the bound alone decides.
A program may use at most 128 MiB of HBM per device.

v0:
```python
import jax
import jax.numpy as jnp
from jax import lax
from jax.sharding import PartitionSpec as P


def inner_product(left, right):
    return lax.dot_general(
        left,
        right,
        (((0,), (0,)), ((), ())),
        precision=lax.Precision.HIGHEST,
        preferred_element_type=jnp.float32,
    )


def on_device(basis, image, coeffs):
    row_block = lax.all_gather(basis, "col", axis=1, tiled=True)
    panel = basis.shape[1]
    columns = row_block
    joined = lax.psum_scatter(
        jnp.concatenate([inner_product(columns, basis), inner_product(columns, image)], axis=1),
        "row",
        scatter_dimension=0,
        tiled=True,
    )
    gram = joined[:, :panel]
    stiffness = joined[:, panel:]
    columns = row_block
    rotated = jnp.dot(
        columns,
        lax.all_gather(coeffs, "row", axis=0, tiled=True),
        precision=lax.Precision.HIGHEST,
        preferred_element_type=jnp.float32,
    )
    return (gram, stiffness, rotated)


def solution(mesh):
    return jax.shard_map(
        on_device,
        mesh=mesh,
        in_specs=(P("row", "col"), P("row", "col"), P("row", "col")),
        out_specs=(P("row", "col"), P("row", "col"), P("row", "col")),
        check_vma=False,
    )
```

profile of v0, /device:TPU:1, one launch (start us, length us, event | category | flops | bytes accessed | tf_op | source)
XLA Modules:
  0.0 404.0 jit_solution(17512835284544326502)
XLA Ops:
  7.2 0.0 copy-start
  7.2 0.0 all-gather.3.cloned.1.call-start
  7.2 0.7 all-gather.3.cloned.1.call-update
  7.9 0.0 all-gather.5.cloned.1.call-start
  8.0 0.7 all-gather.5.cloned.1.call-update
  8.7 0.0 reduce-scatter.2.cloned.1.call-start
  8.7 145.2 %all-gather.3.cloned.1.call-done = f32[256,6144]{1,0:T(8,128)} async-done(((f32[256,384]{1,0:T(8,128)}), f32[256,6144]{1,0:T(8,128)}) %all-gather.3.cloned.1.call-update) | async-done | bytes 6291472 | tf_op jit(solution)/shard_map/all_gather | solution.py:18
  154.0 0.0 copy-start.1
  154.0 11.0 %fusion.1 = f32[6144,384]{0,1:T(8,128)S(1)} fusion(f32[256,6144]{1,0:T(8,128)} %all-gather.3.cloned.1.call-done, f32[256,384]{1,0:T(8,128)} %param.3), kind=kOutput, calls=%fused_computation.2 | convolution fusion | flops 7247757312 | bytes 16121856 | tf_op jit(solution)/shard_map/dot_general | solution.py:8
  165.0 0.0 copy-done
  165.0 0.0 copy-done.1
  165.0 8.9 %fusion.2 = f32[6144,384]{0,1:T(8,128)S(1)} fusion(f32[256,6144]{1,0:T(8,128)S(1)} %copy-done.1, f32[256,384]{1,0:T(8,128)S(1)} %copy-done), kind=kOutput, calls=%fused_computation.3 | convolution fusion | flops 7247757312 | bytes 16121856 | tf_op jit(solution)/shard_map/dot_general | solution.py:8
  173.9 7.0 %pad_maximum_fusion = f32[6144,768]{0,1:T(8,128)} fusion(f32[6144,384]{0,1:T(8,128)S(1)} %fusion.2, f32[6144,384]{0,1:T(8,128)S(1)} %fusion.1), kind=kLoop, calls=%fused_computation | loop fusion | flops 4718592 | bytes 37748736 | tf_op jit(solution)/shard_map/concatenate | solution.py:22
  180.9 0.0 reduce-scatter.2.cloned.1.call-update
  180.9 46.3 %all-gather.5.cloned.1.call-done = f32[6144,256]{1,0:T(8,128)} async-done(((f32[384,256]{1,0:T(8,128)}), f32[6144,256]{1,0:T(8,128)}) %all-gather.5.cloned.1.call-update) | async-done | bytes 6291472 | tf_op jit(solution)/shard_map/all_gather | solution.py:32
  227.3 10.5 %fusion.3 = f32[256,256]{1,0:T(8,128)} fusion(f32[256,6144]{1,0:T(8,128)} %all-gather.3.cloned.1.call-done, f32[6144,256]{1,0:T(8,128)} %all-gather.5.cloned.1.call-done), kind=kOutput, calls=%fused_computation.4 | convolution fusion | flops 4831838208 | bytes 12845056 | tf_op jit(solution)/shard_map/dot_general | solution.py:30
  237.8 156.3 %reduce-scatter.2.cloned.1.call-done = f32[384,768]{0,1:T(8,128)} async-done(((f32[6144,768]{0,1:T(8,128)}), f32[384,768]{0,1:T(8,128)}) %reduce-scatter.2.cloned.1.call-update) | async-done | bytes 1179664 | tf_op jit(solution)/shard_map/reduce_scatter | solution.py:21
  394.1 1.3 fusion
  395.4 1.1 copy.7
  396.5 1.0 copy.6
Async XLA Ops:
  7.2 157.8 %copy-start = (f32[256,384]{1,0:T(8,128)S(1)}, f32[256,384]{1,0:T(8,128)}, u32[]{:S(2)}) copy-start(f32[256,384]{1,0:T(8,128)} %param.4) | copy-start | bytes 1179652
  7.2 146.8 %all-gather.3.cloned.1.call-start = ((), (), s32[]{:S(2)}) async-start(), calls=%async_computation.1 | async-start | bytes 6684672 | tf_op jit(solution)/shard_map/all_gather | solution.py:18
  7.9 219.3 %all-gather.5.cloned.1.call-start = ((), (), s32[]{:S(2)}) async-start(), calls=%async_computation.3 | async-start | bytes 6684672 | tf_op jit(solution)/shard_map/all_gather | solution.py:32
  8.7 385.4 %reduce-scatter.2.cloned.1.call-start = ((), (), s32[]{:S(2)}) async-start(), calls=%async_computation.2 | async-start | bytes 20054016 | tf_op jit(solution)/shard_map/reduce_scatter | solution.py:21
  154.0 11.0 %copy-start.1 = (f32[256,6144]{1,0:T(8,128)S(1)}, f32[256,6144]{1,0:T(8,128)}, u32[]{:S(2)}) copy-start(f32[256,6144]{1,0:T(8,128)} %all-gather.3.cloned.1.call-done) | copy-start | bytes 18874372
Sparse Core Ops, SparseCore 0:
  9.8 144.0 all-gather.2
  156.7 70.4 all-gather.4
  231.9 162.1 reduce-scatter.1
where the time goes:
time: 404 us
  waiting for transfers between devices  349 us (86%)
  matrix products  30.5 us (8%)
  between operations  13.8 us (3%)
  other arithmetic  7.01 us (2%)
    reduce_scatter x1, waiting for transfers between devices, on_device(): lax.psum_scatter(jnp.concatenate([inner_product(columns, basis), inner_pr...  156 us
    all_gather x1, waiting for transfers between devices, on_device(): row_block = lax.all_gather(basis, 'col', axis=1, tiled=True)  145 us
    all_gather x1, waiting for transfers between devices, on_device(): lax.all_gather(coeffs, 'row', axis=0, tiled=True)  46.3 us
    dot_general x2, matrix products, inner_product(): lax.dot_general(left, right, (((0,), (0,)), ((), ())), precision=lax.Prec...  19.9 us
    dot_general x1, matrix products, on_device(): jnp.dot(columns, lax.all_gather(coeffs, 'row', axis=0, tiled=True), preci...  10.5 us
  transfers between devices with their start and end apart: 3, of which 3 were waited for; matrix products, arithmetic and copies ran while one was open for 9% of the time, Pallas kernels for 0%

commit v1 on v0

v1 whole, which is shorter than its diff:
```python
import functools

import jax
import jax.numpy as jnp
from jax import lax
from jax.experimental import pallas as pl
from jax.experimental.pallas import tpu as pltpu
from jax.sharding import PartitionSpec as P

MESH = pl.DeviceIdType.MESH
F32, BF16 = jnp.float32, jnp.bfloat16
NY, NZ = 4, 8
RB, CB, OB = 256, 384, 256
NB = 8
NM, MW = 3, 128
STEPS = NM * NB
LAG = 2


def halves(v):
    hi = v.astype(BF16)
    return hi, (v - hi.astype(F32)).astype(BF16)


def dot(a, b):
    return jnp.dot(a, b, preferred_element_type=F32)


def kernel(
    basis, image, coeffs, gram, stiff, rot,
    lbuf, rbuf, rt_hi, rt_lo, cbuf, c_hi, c_lo, l_hi, l_lo, pbuf, precv, rotp, rotc, rots, roty,
    l_recv, l_send, z_send, r_recv, r_send, c_recv, c_send, p_recv, p_send, rc_recv, rc_send, ry_recv, ry_send,
):
    row, col = lax.axis_index("row"), lax.axis_index("col")
    xh, y, core = lax.div(row, 8), lax.rem(lax.div(row, 2), 4), lax.rem(row, 2)
    z, xl = lax.div(col, 2), lax.rem(col, 2)
    zs = lax.rem(z, 4)
    d = lax.rem(z - y + NZ, 4)
    own_blk = y * 2 + core

    def dev(dxh=0, dxl=0, dy=0, dz=0, dc=0):
        a, b = lax.rem(xh + dxh, 2), lax.rem(xl + dxl, 2)
        return (a * 8 + lax.rem(y + dy + NY, NY) * 2 + lax.rem(core + dc, 2), lax.rem(z + dz + NZ, NZ) * 2 + b)

    other_core, partner = dev(dc=1), dev(dxh=1)
    y_up, y_dn, z_up, z_dn = dev(dy=1), dev(dy=-1), dev(dz=1), dev(dz=-1)

    def send(src, dst, s, r, to):
        return pltpu.make_async_remote_copy(
            src_ref=src, dst_ref=dst, send_sem=s, recv_sem=r, device_id=to, device_id_type=MESH
        )

    def arrived(dst, r):
        send(dst, dst, l_send.at[0, 0], r, other_core).wait_recv()

    barrier = pltpu.get_barrier_semaphore()
    peers = [dev(dxl=a, dy=b, dc=c) for a in range(2) for b in range(4) for c in range(2) if a + b + c]
    peers += [z_up, z_dn, partner]
    for p in peers:
        pl.semaphore_signal(barrier, inc=1, device_id=p, device_id_type=MESH)
    pl.semaphore_wait(barrier, len(peers))

    def gather(m, a):
        to = (xh * 8 + zs * 2 + xl, z * 2 + lax.rem(xl + a, 2))
        return send(
            basis.at[:, pl.ds(m * MW, MW)], lbuf.at[m, 0, own_blk], l_send.at[m, a], l_recv.at[m, 0, own_blk], to
        )

    mine = (y == zs) & (core == xl)

    def gather_start(m):
        @pl.when(mine)
        def _():
            pltpu.make_async_copy(
                basis.at[:, pl.ds(m * MW, MW)], lbuf.at[m, 0, own_blk], l_recv.at[m, 0, own_blk]
            ).start()

        @pl.when(jnp.logical_not(mine))
        def _():
            gather(m, 0).start()

        gather(m, 1).start()

    for m in range(NM):
        gather_start(m)

    sends = []

    def r_go(arr, blk, to, src=None):
        cp = send(
            rbuf.at[arr, blk] if src is None else src, rbuf.at[arr, blk], r_send.at[len(sends)], r_recv.at[arr, blk], to
        )
        cp.start()
        sends.append(cp)

    for arr, src in enumerate((basis, image)):
        pltpu.make_async_copy(src, rbuf.at[arr, own_blk], r_recv.at[arr, own_blk]).start()
        r_go(arr, own_blk, y_up, src)
        r_go(arr, own_blk, y_dn, src)
        r_go(arr, own_blk, other_core, src)

    own_c = pltpu.make_async_copy(coeffs, cbuf.at[xh], c_send.at[1])
    own_c.start()
    c_cp = send(coeffs, cbuf.at[xh], c_send.at[0], c_recv, partner)
    c_cp.start()

    def blk_of(dy, c):
        return lax.rem(y + dy, NY) * 2 + c

    def chunk(i):
        m, j = lax.div(i, NB), lax.rem(i, NB)
        q, c = lax.div(j, 2), lax.rem(j, 2)
        dy = jnp.where(q == 2, 3, jnp.where(q == 3, 2, q))
        return m, c, blk_of(dy, c)

    def z_copy(i, slot, m, blk, up):
        if up:
            to, into = z_up, jnp.where(d == 3, 1, 0)
        else:
            to, into = z_dn, 1
        return send(
            lbuf.at[m, slot, blk], lbuf.at[m, into, blk], z_send.at[0 if up else 1, i], l_recv.at[m, into, blk], to
        )

    def step_a(i, wait):
        m, c, blk = chunk(i)
        if not wait:
            arrived(lbuf.at[m, 0, blk], l_recv.at[m, 0, blk])

        @pl.when((d < 3) | (c == 0))
        def _():
            cp = z_copy(i, 0, m, blk, True)
            cp.wait_send() if wait else cp.start()

        @pl.when(d == 0)
        def _():
            cp = z_copy(i, 0, m, blk, False)
            cp.wait_send() if wait else cp.start()

    def step_b(i, wait):
        m, c, blk = chunk(i)
        if not wait:
            arrived(lbuf.at[m, 1, blk], l_recv.at[m, 1, blk])

        @pl.when((d > 1) | ((d == 1) & (c == 1)))
        def _():
            cp = z_copy(i, 1, m, blk, False)
            cp.wait_send() if wait else cp.start()

    def step(t):
        ia, ib = t - LAG * d, t - LAG * (4 - d)

        @pl.when((ia >= 0) & (ia < STEPS))
        def _():
            step_a(ia, False)

        @pl.when((ib >= 0) & (ib < STEPS))
        def _():
            step_b(ib, False)

    def loop(lo, hi, body):
        def go(t, carry):
            body(t)
            return carry

        lax.fori_loop(lo, hi, go, 0)

    def transpose(blk):
        for arr in range(2):
            arrived(rbuf.at[arr, blk], r_recv.at[arr, blk])
            hi, lo = halves(rbuf[arr, blk].T)
            at = (pl.ds(arr * CB, CB), pl.ds(pl.multiple_of(blk * RB, RB), RB))
            rt_hi[at] = hi
            rt_lo[at] = lo

    own = jnp.where(lax.div(lax.rem(z - d + NZ, NZ), 4) == xh, 0, 1)
    h_a = jnp.where(own == 0, xh, 1 - xh)

    def split_l(m, blks):
        for b in blks:
            at = pl.ds(b * RB, RB)
            for slot in range(2):
                hi, lo = halves(lbuf[m, slot, b])
                l_hi[at, pl.ds(slot * MW, MW)] = hi
                l_lo[at, pl.ds(slot * MW, MW)] = lo

    def grams(m, arr):
        at = pl.ds(arr * CB, CB)
        acc = dot(rt_hi[at, :], l_hi[...]) + dot(rt_hi[at, :], l_lo[...]) + dot(rt_lo[at, :], l_hi[...])
        pbuf[m, :, at] = acc.T

    def p_copy(m):
        src = pbuf.at[m, pl.ds(pl.multiple_of((1 - own) * MW, MW), MW)]
        return send(src, precv.at[m], p_send.at[m], p_recv.at[m], partner)

    def rotate(m, b):
        at = pl.ds(b * RB, RB)
        a_hi, a_lo = l_hi[at, :], l_lo[at, :]
        acc = dot(a_hi, c_hi[m]) + dot(a_hi, c_lo[m]) + dot(a_lo, c_hi[m])
        rotp[b] = acc if m == 0 else rotp[b] + acc

    loop(0, 13, step)

    for arr in range(2):
        for dy in (1, 3):
            blk = blk_of(dy, core)
            arrived(rbuf.at[arr, blk], r_recv.at[arr, blk])
            r_go(arr, blk, other_core)
            if (arr, dy) == (0, 3):
                r_go(arr, blk, y_up)
            if (arr, dy) == (1, 1):
                r_go(arr, blk, y_dn)

    def transpose_ready(blk):
        for arr in range(2):
            hi, lo = halves(rbuf[arr, blk].T)
            at = (pl.ds(arr * CB, CB), pl.ds(pl.multiple_of(blk * RB, RB), RB))
            rt_hi[at] = hi
            rt_lo[at] = lo

    def with_step(t, *work):
        step(jnp.int32(t))
        for f in work:
            f()

    def split_c():
        own_c.wait()
        arrived(cbuf.at[1 - xh], c_recv)
        for m in range(NM):
            for slot in range(2):
                h = h_a if slot == 0 else 1 - h_a
                hi, lo = halves(cbuf[h, pl.ds(m * MW, MW), :])
                c_hi[m, pl.ds(slot * MW, MW), :] = hi
                c_lo[m, pl.ds(slot * MW, MW), :] = lo

    with_step(13, lambda: transpose(blk_of(0, core)))
    with_step(14, lambda: transpose(blk_of(0, 1 - core)))
    with_step(15, lambda: transpose_ready(blk_of(1, core)))
    with_step(16, lambda: transpose_ready(blk_of(3, core)))
    with_step(17, lambda: transpose(blk_of(1, 1 - core)))
    with_step(18, lambda: transpose(blk_of(3, 1 - core)))
    with_step(19, split_c)
    blk = blk_of(2, core)
    for arr in range(2):
        arrived(rbuf.at[arr, blk], r_recv.at[arr, blk])
        r_go(arr, blk, other_core)
    with_step(20, lambda: transpose_ready(blk))
    with_step(21, lambda: transpose(blk_of(2, 1 - core)))

    def rot_some(m, blks):
        for b in blks:
            rotate(m, b)

    with_step(22, lambda: split_l(0, range(8)))
    with_step(23, lambda: grams(0, 0))
    with_step(24, lambda: grams(0, 1), lambda: p_copy(0).start())
    with_step(25, lambda: rot_some(0, range(8)))
    with_step(26, lambda: split_l(1, range(8)))
    with_step(27, lambda: grams(1, 0))
    with_step(28, lambda: grams(1, 1), lambda: p_copy(1).start())
    with_step(29, lambda: rot_some(1, range(8)))
    loop(30, STEPS + 4 * LAG, step)

    split_l(2, range(8))
    rot_some(2, range(8))
    rc = [
        send(rotp.at[b * 2 + 1 - core], rotc.at[b], rc_send.at[b], rc_recv.at[b], other_core) for b in range(NY)
    ]
    for cp in rc:
        cp.start()
    grams(2, 0)
    grams(2, 1)
    p_copy(2).start()
    for cp in rc:
        cp.wait()
    for b in range(NY):
        rots[b] = rotp[b * 2 + core] + rotc[b]
    ry = []
    for o in (2, 1, 3):
        cp = send(rots.at[lax.rem(y + o, NY)], roty.at[o - 1], ry_send.at[o - 1], ry_recv.at[o - 1], dev(dy=o))
        cp.start()
        ry.append(cp)

    at_own = pl.ds(pl.multiple_of(own * MW, MW), MW)
    for m in range(NM):
        p_copy(m).wait()
        rows = pl.ds(m * MW, MW)
        gram[rows, :] = pbuf[m, at_own, pl.ds(0, CB)] + precv[m, :, pl.ds(0, CB)]
        stiff[rows, :] = pbuf[m, at_own, pl.ds(CB, CB)] + precv[m, :, pl.ds(CB, CB)]
    for cp in ry:
        cp.wait()
    rot[...] = rots[y] + roty[0] + roty[1] + roty[2]

    for m in range(NM):
        pl.when(jnp.logical_not(mine))(gather(m, 0).wait_send)
        gather(m, 1).wait_send()
    for cp in sends:
        cp.wait_send()
    c_cp.wait_send()

    def drain(i):
        step_a(i, True)
        step_b(i, True)

    loop(0, STEPS, drain)


def on_device(basis, image, coeffs):
    dma = pltpu.SemaphoreType.DMA
    return pl.pallas_call(
        kernel,
        out_shape=[
            jax.ShapeDtypeStruct((CB, CB), F32),
            jax.ShapeDtypeStruct((CB, CB), F32),
            jax.ShapeDtypeStruct((RB, OB), F32),
        ],
        in_specs=[pl.BlockSpec(memory_space=pltpu.VMEM)] * 3,
        out_specs=[pl.BlockSpec(memory_space=pltpu.VMEM)] * 3,
        scratch_shapes=[
            pltpu.VMEM((NM, 2, NB, RB, MW), F32),
            pltpu.VMEM((2, NB, RB, CB), F32),
            pltpu.VMEM((2 * CB, NB * RB), BF16),
            pltpu.VMEM((2 * CB, NB * RB), BF16),
            pltpu.VMEM((2, CB, OB), F32),
            pltpu.VMEM((NM, 2 * MW, OB), BF16),
            pltpu.VMEM((NM, 2 * MW, OB), BF16),
            pltpu.VMEM((NB * RB, 2 * MW), BF16),
            pltpu.VMEM((NB * RB, 2 * MW), BF16),
            pltpu.VMEM((NM, 2 * MW, 2 * CB), F32),
            pltpu.VMEM((NM, MW, 2 * CB), F32),
            pltpu.VMEM((NB, RB, OB), F32),
            pltpu.VMEM((NY, RB, OB), F32),
            pltpu.VMEM((NY, RB, OB), F32),
            pltpu.VMEM((NY - 1, RB, OB), F32),
            dma((NM, 2, NB)),
            dma((NM, 2)),
            dma((2, STEPS)),
            dma((2, NB)),
            dma((16,)),
            dma,
            dma((2,)),
            dma((NM,)),
            dma((NM,)),
            dma((NY,)),
            dma((NY,)),
            dma((NY - 1,)),
            dma((NY - 1,)),
        ],
        compiler_params=pltpu.CompilerParams(
            collective_id=0, has_side_effects=True, vmem_limit_bytes=56 * 2**20
        ),
        cost_estimate=pl.CostEstimate(flops=2 * 1610612736 * 3, bytes_accessed=4 * 2**20, transcendentals=0),
    )(basis, image, coeffs)


def solution(mesh):
    return jax.shard_map(
        on_device,
        mesh=mesh,
        in_specs=(P("row", "col"),) * 3,
        out_specs=(P("row", "col"),) * 3,
        check_vma=False,
    )
```

time: 404 us -> 135 us (0.33)
  waiting for transfers between devices: 349 us -> 0 us
  Pallas kernels: 0 us -> 129 us
  matrix products: 30.5 us -> 0 us
  between operations: 13.8 us -> 0.65 us
  other arithmetic: 7.01 us -> 0 us
    all_gather x2 -> x0, waiting for transfers between devices: 192 us -> none  [the longest x1 145 us: on_device(): row_block = lax.all_gather(basis, 'col', axis=1, tiled=True)]
    reduce_scatter x1 -> x0, waiting for transfers between devices: 156 us -> none  [on_device(): lax.psum_scatter(jnp.concatenate([inner_product(columns, basis), inner_pr...]
    pallas_call x0 -> x1, Pallas kernels: none -> 129 us  [on_device(): pl.pallas_call(kernel, out_shape=[jax.ShapeDtypeStruct((CB, CB), F32), ja...]
    dot_general x3 -> x0, matrix products: 30.5 us -> none  [the longest x2 19.9 us: inner_product(): lax.dot_general(left, right, (((0,), (0,)), ((), ())), precision=lax.Prec...]
    concatenate x1 -> x0, other arithmetic: 7.01 us -> none  [on_device(): jnp.concatenate([inner_product(columns, basis), inner_product(columns, im...]
  transfers between devices with their start and end apart: 3 -> 0, of which waited for: 3 -> 0; matrix products, arithmetic and copies ran while one was open for 9% -> 0% of each run, Pallas kernels for 0% -> 0%
where the time goes in v1:
time: 135 us; the launch traced here: 134 us
  Pallas kernels  129 us (96%)
  local copies, waits for them, and re-layouts  3.78 us (3%)
    pallas_call x1, Pallas kernels, on_device(): pl.pallas_call(kernel, out_shape=[jax.ShapeDtypeStruct((CB, CB), F32), ja...  129 us
    unnamed x7, local copies, waits for them, and re-layouts  3.78 us

profile of v1, /device:TPU:1, one launch (start us, length us, event | category | flops | bytes accessed | tf_op | source)
XLA Modules:
  0.0 133.8 jit_solution(13891274433066226242)
XLA Ops:
  0.6 129.4 %shard_map.58 = (f32[384,384]{1,0:T(8,128)}, f32[384,384]{1,0:T(8,128)}, f32[256,256]{1,0:T(8,128)}) custom-call(f32[256,384]{1,0:T(8,128)} %basis.1, f32[256,384]{1,0:T(8,128)} %image.1, f32[384,256]{1,0:T(8,128)} %coeffs.1), custom_call_target="tpu_custom_call" | custom-call | flops 9663676416 | bytes 4194304 | tf_op jit(solution)/shard_map/pallas_call | solution.py:310
  130.1 0.0 copy-start
  130.1 2.0 %copy.9 = f32[384,384]{1,0:T(8,128)} copy(f32[384,384]{1,0:T(8,128)} %get-tuple-element.6) | data formatting | bytes 1179648
  132.0 0.0 copy-done
  132.0 0.0 copy-start.1
  132.0 0.8 copy.10
  132.9 0.3 copy-done.1
  133.1 0.7 copy.11
Async XLA Ops:
  130.1 2.0 %copy-start = (f32[384,384]{1,0:T(8,128)S(1)}, f32[384,384]{1,0:T(8,128)}, u32[]{:S(2)}) copy-start(f32[384,384]{1,0:T(8,128)} %get-tuple-element.7) | copy-start | bytes 1769476
  132.0 1.1 copy-start.1

commit v2 on v0

v2 whole, which is shorter than its diff:
```python
import functools

import jax
import jax.numpy as jnp
from jax import lax
from jax.experimental import pallas as pl
from jax.experimental.pallas import tpu as pltpu
from jax.sharding import PartitionSpec as P

MESH = pl.DeviceIdType.MESH
F32, BF16 = jnp.float32, jnp.bfloat16
NY, NZ = 4, 8
RB, CB, OB = 256, 384, 256
NB = 8
NG, GW = 6, 64
UNIT = 4
UNITS = NG * NB // UNIT
LAG = 1
END = UNITS + 4 * LAG
R_NEAR, R_FAR = 7, 9
SHARED = 2


def halves(v):
    hi = v.astype(BF16)
    return hi, (v - hi.astype(F32)).astype(BF16)


def dot(a, b):
    return jnp.dot(a, b, preferred_element_type=F32)


def loop(lo, hi, body):
    def go(t, carry):
        body(t)
        return carry

    lax.fori_loop(lo, hi, go, 0)


def kernel(
    basis, image, coeffs, gram, stiff, rot,
    bt, lbuf, rbuf, r_hi, r_lo, cbuf, c_hi, c_lo, l_hi, l_lo, pbuf, precv, rotp, rotc, rots, roty,
    l_recv, l_send, z_send, x_send, r_recv, r_send, c_recv, c_send, p_recv, p_send, rc_recv, rc_send, ry_recv, ry_send,
):
    row, col = lax.axis_index("row"), lax.axis_index("col")
    xh, y, core = lax.div(row, 8), lax.rem(lax.div(row, 2), 4), lax.rem(row, 2)
    z, xl = lax.div(col, 2), lax.rem(col, 2)
    zs = lax.rem(z, 4)
    d = lax.rem(z - y + NZ, 4)
    own_blk = y * 2 + core
    lead = core == xl

    def dev(dxh=0, dxl=0, dy=0, dz=0, dc=0):
        a, b = lax.rem(xh + dxh, 2), lax.rem(xl + dxl, 2)
        return (a * 8 + lax.rem(y + dy + NY, NY) * 2 + lax.rem(core + dc, 2), lax.rem(z + dz + NZ, NZ) * 2 + b)

    other_core, partner, x_pair = dev(dc=1), dev(dxh=1), dev(dxl=1)
    y_up, y_dn, z_up, z_dn = dev(dy=1), dev(dy=-1), dev(dz=1), dev(dz=-1)

    def send(src, dst, s, r, to):
        return pltpu.make_async_remote_copy(
            src_ref=src, dst_ref=dst, send_sem=s, recv_sem=r, device_id=to, device_id_type=MESH
        )

    def arrived(dst, r):
        send(dst, dst, l_send.at[0], r, other_core).wait_recv()

    barrier = pltpu.get_barrier_semaphore()
    peers = [dev(dxl=a, dy=b, dc=c) for a in range(2) for b in range(4) for c in range(2) if a + b + c]
    peers += [z_up, z_dn, partner]
    for p in peers:
        pl.semaphore_signal(barrier, inc=1, device_id=p, device_id_type=MESH)
    own_in = [
        pltpu.make_async_copy(src, rbuf.at[arr, own_blk], r_recv.at[arr, own_blk])
        for arr, src in enumerate((basis, image))
    ]
    own_in.append(pltpu.make_async_copy(coeffs, cbuf.at[xh], c_send.at[1]))
    for cp in own_in:
        cp.start()
    own_in[0].wait()
    bt[...] = rbuf[0, own_blk].T
    own_in[1].wait()
    pl.semaphore_wait(barrier, len(peers))

    def blk_of(dy, c):
        return lax.rem(y + dy, NY) * 2 + c

    dy_src = lax.rem(y - zs + NY, NY)
    shared_src = ((dy_src == 1) | (dy_src == 2)) & (core == 0)
    mine = (y == zs) & lead

    def gather(g):
        src, dst, r = bt.at[pl.ds(g * GW, GW)], lbuf.at[0, own_blk, pl.ds(g * GW, GW)], l_recv.at[g, 0, own_blk]
        to = (xh * 8 + zs * 2 + xl, z * 2 + xl)
        pl.when(mine)(pltpu.make_async_copy(src, dst, r).start)
        pl.when(jnp.logical_not(mine))(send(src, dst, l_send.at[0], r, to).start)
        to = (xh * 8 + zs * 2 + xl, z * 2 + 1 - xl)
        if g < NG - 1:
            pl.when(jnp.logical_not(shared_src))(send(src, dst, l_send.at[1], r, to).start)
        else:
            send(src, dst, l_send.at[1], r, to).start()

    sends = []

    def r_go(arr, blk, to):
        at = rbuf.at[arr, blk]
        cp = send(at, at, r_send.at[len(sends)], r_recv.at[arr, blk], to)
        cp.start()
        sends.append(cp)

    def r_start(arr):
        r_go(arr, own_blk, y_up)
        r_go(arr, own_blk, y_dn)
        r_go(arr, own_blk, other_core)

    c_cp = send(coeffs, cbuf.at[xh], c_send.at[0], c_recv, partner)
    gather(0)
    gather(1)
    r_start(0)
    gather(2)
    r_start(1)
    gather(3)
    gather(4)
    gather(5)
    c_cp.start()

    def chunk_ref(g, slot, blk):
        return lbuf.at[slot, blk, pl.ds(pl.multiple_of(g * GW, GW), GW)]

    def pass_on(u, k, slot):
        g, half = lax.div(u, 2), lax.rem(u, 2)
        c = k % 2
        blk = blk_of(jnp.where(half == 0, k // 2, 3 - k // 2), c)
        src = chunk_ref(g, slot, blk)

        def along_z(up):
            into = jnp.where(d == 3, 1, 0) if up else 1
            send(
                src, chunk_ref(g, into, blk), z_send.at[0 if up else 1, g], l_recv.at[g, into, blk], z_up if up else z_dn
            ).start()

        def from_z():
            arrived(src, l_recv.at[g, slot, blk])
            if slot == 0:
                along_z(True) if c == 0 else pl.when(d < 3)(lambda: along_z(True))
                pl.when(d == 0)(lambda: along_z(False))
            else:
                pl.when((d > 1) | (d == 1) if c == 1 else d > 1)(lambda: along_z(False))

        if k == SHARED:
            pl.when(lead | (g == NG - 1))(from_z)
            pl.when(lead & (g < NG - 1))(send(src, src, x_send.at[g], l_recv.at[g, slot, blk], x_pair).start)
        else:
            from_z()

    def step(t, k):
        ua, ub = t - LAG * d, t - LAG * (4 - d)
        pl.when((ua >= 0) & (ua < UNITS))(lambda: pass_on(ua, k, 0))
        pl.when((ub >= 0) & (ub < UNITS))(lambda: pass_on(ub, k, 1))

    def unit(t):
        for k in range(UNIT):
            step(t, k)

    def sent(n, s):
        at = lbuf.at[0, pl.ds(0, n), pl.ds(0, GW)]
        send(at, at, s, l_recv.at[0, 0, 0], other_core).wait_send()

    def drain():
        for g in range(NG):
            few = g < NG - 1
            for up in (True, False):
                s = z_send.at[0 if up else 1, g]
                part = d == 3 if up else d == 1
                whole = jnp.logical_not(part)
                if few:
                    pl.when(whole & lead)(lambda: sent(8, s))
                    pl.when(whole & jnp.logical_not(lead))(lambda: sent(6, s))
                else:
                    pl.when(whole)(lambda: sent(8, s))
                if few and up:
                    pl.when(part & lead)(lambda: sent(4, s))
                    pl.when(part & jnp.logical_not(lead))(lambda: sent(2, s))
                else:
                    pl.when(part)(lambda: sent(4, s))
            if few:
                pl.when(lead)(lambda: sent(4, x_send.at[g]))

    own = jnp.where(lax.div(lax.rem(z - d + NZ, NZ), 4) == xh, 0, 1)
    h_a = jnp.where(own == 0, xh, 1 - xh)

    def split_r(blk, wait=True):
        for arr in range(2):
            if wait:
                arrived(rbuf.at[arr, blk], r_recv.at[arr, blk])
            hi, lo = halves(rbuf[arr, blk])
            at = (pl.ds(pl.multiple_of(blk * RB, RB), RB), pl.ds(arr * CB, CB))
            r_hi[at] = hi
            r_lo[at] = lo

    def split_c():
        own_in[2].wait()
        arrived(cbuf.at[1 - xh], c_recv)
        for g in range(NG):
            rows = pl.ds(g * GW, GW)
            both = jnp.concatenate([cbuf[h_a, rows, :], cbuf[1 - h_a, rows, :]], axis=0)
            hi, lo = halves(both.T)
            c_hi[:, pl.ds(g * 2 * GW, 2 * GW)] = hi
            c_lo[:, pl.ds(g * 2 * GW, 2 * GW)] = lo

    def shared_arrived(g):
        @pl.when(jnp.logical_not(lead))
        def _():
            for dy in (1, 2):
                blk = blk_of(dy, 0)
                for slot in range(2):
                    arrived(chunk_ref(g, slot, blk), l_recv.at[g, slot, blk])

    def split_l(groups, blks):
        for b in blks:
            cols = pl.ds(b * RB, RB)
            for k, g in enumerate(groups):
                for slot in range(2):
                    hi, lo = halves(lbuf[slot, b, pl.ds(g * GW, GW), :])
                    rows = pl.ds((k * 2 + slot) * GW, GW)
                    l_hi[rows, cols] = hi
                    l_lo[rows, cols] = lo

    def grams(groups, n):
        cols, rows = pl.ds(n * 256, 256), pl.ds(0, len(groups) * 2 * GW)
        a_hi, b_hi = l_hi[rows, :], r_hi[:, cols]
        acc = dot(a_hi, b_hi) + dot(l_lo[rows, :], b_hi) + dot(a_hi, r_lo[:, cols])
        for k, g in enumerate(groups):
            for slot in range(2):
                at = (k * 2 + slot) * GW
                pbuf[g, slot, :, cols] = acc[at : at + GW, :]

    def grams_part(g, n, part, dys):
        cols, rows, acc = pl.ds(n * 256, 256), pl.ds(0, 2 * GW), 0.0
        for dy in dys:
            ks = pl.ds(pl.multiple_of(lax.rem(y + dy, NY) * 2 * RB, 2 * RB), 2 * RB)
            a_hi, b_hi = l_hi[rows, ks], r_hi[ks, cols]
            acc += dot(a_hi, b_hi) + dot(l_lo[rows, ks], b_hi) + dot(a_hi, r_lo[ks, cols])
        for slot in range(2):
            v = acc[slot * GW : slot * GW + GW, :]
            pbuf[g, slot, :, cols] = v if part == 0 else pbuf[g, slot, :, cols] + v

    def split_part(g, dys):
        for dy in dys:
            for c in range(2):
                b = blk_of(dy, c)
                cols = pl.ds(pl.multiple_of(b * RB, RB), RB)
                for slot in range(2):
                    hi, lo = halves(lbuf[slot, b, pl.ds(g * GW, GW), :])
                    l_hi[pl.ds(slot * GW, GW), cols] = hi
                    l_lo[pl.ds(slot * GW, GW), cols] = lo

    def rotate_part(g, dys):
        rows, ks = pl.ds(0, 2 * GW), pl.ds(g * 2 * GW, 2 * GW)
        for dy in dys:
            for c in range(2):
                b = blk_of(dy, c)
                cols = pl.ds(pl.multiple_of(b * RB, RB), RB)
                b_hi, b_lo = l_hi[rows, cols], l_lo[rows, cols]
                rotp[b] += dot(c_hi[:, ks], b_hi) + dot(c_lo[:, ks], b_hi) + dot(c_hi[:, ks], b_lo)

    def p_copy(g):
        return send(pbuf.at[g, 1 - own], precv.at[g], p_send.at[g], p_recv.at[g], partner)

    def rotate(groups, blks):
        rows = pl.ds(0, len(groups) * 2 * GW)
        ks = pl.ds(groups[0] * 2 * GW, len(groups) * 2 * GW)
        for b in blks:
            cols = pl.ds(b * RB, RB)
            b_hi, b_lo = l_hi[rows, cols], l_lo[rows, cols]
            acc = dot(c_hi[:, ks], b_hi) + dot(c_lo[:, ks], b_hi) + dot(c_hi[:, ks], b_lo)
            rotp[b] = acc if groups[0] == 0 else rotp[b] + acc

    def p_go(groups):
        for g in groups:
            p_copy(g).start()

    def r_near():
        for arr in range(2):
            for dy in (1, 3):
                blk = blk_of(dy, core)
                arrived(rbuf.at[arr, blk], r_recv.at[arr, blk])
                r_go(arr, blk, other_core)
                if (arr, dy) == (0, 3):
                    r_go(arr, blk, y_up)
                if (arr, dy) == (1, 1):
                    r_go(arr, blk, y_dn)

    def r_far():
        blk = blk_of(2, core)
        for arr in range(2):
            arrived(rbuf.at[arr, blk], r_recv.at[arr, blk])
            r_go(arr, blk, other_core)

    rc, ry = {}, {}

    def rc_go(dys):
        for dy in dys:
            b = lax.rem(y + dy, NY)
            rc[dy] = send(rotp.at[b * 2 + 1 - core], rotc.at[b], rc_send.at[dy], rc_recv.at[dy], other_core)
            rc[dy].start()

    def ry_go(dys):
        for dy in dys:
            rc[dy].wait()
            b = lax.rem(y + dy, NY)
            rots[b] = rotp[b * 2 + core] + rotc[b]
            if dy:
                ry[dy] = send(rots.at[b], roty.at[dy - 1], ry_send.at[dy - 1], ry_recv.at[dy - 1], dev(dy=dy))
                ry[dy].start()

    def pair_work(groups):
        yield lambda: [shared_arrived(g) for g in groups if g < NG - 1] and split_l(groups, range(4))
        yield lambda: split_l(groups, range(4, 8))
        yield lambda: grams(groups, 0)
        yield lambda: grams(groups, 1)
        yield lambda: grams(groups, 2)
        yield lambda: p_go(groups)
        yield lambda: rotate(groups, range(4))
        yield lambda: rotate(groups, range(4, 8))

    plan = {}

    def at(t, *work):
        n = t * UNIT
        for w in work:
            while n in plan:
                n += 1
            plan[n] = w

    at(
        R_NEAR,
        r_near,
        lambda: split_r(blk_of(0, core), False),
        lambda: split_r(blk_of(0, 1 - core)),
        lambda: split_r(blk_of(1, core), False),
        lambda: split_r(blk_of(3, core), False),
        lambda: split_r(blk_of(1, 1 - core)),
        lambda: split_r(blk_of(3, 1 - core)),
        split_c,
    )
    at(R_FAR, r_far, lambda: split_r(blk_of(2, core), False), lambda: split_r(blk_of(2, 1 - core)))
    at(max(R_FAR, 4 + 4 * LAG), *pair_work((0, 1)))
    at(8 + 4 * LAG, *pair_work((2, 3)))
    at(10 + 4 * LAG, *pair_work((4,)))
    first, second = (0, 1), (3, 2)
    at(
        11 + 4 * LAG,
        lambda: split_part(5, first),
        lambda: rotate_part(5, first),
        lambda: [rc_go(first), grams_part(5, 0, 0, first)],
        lambda: [ry_go(first), grams_part(5, 1, 0, first)],
    )
    loop(0, R_NEAR, unit)
    for n in range(R_NEAR * UNIT, END * UNIT):
        step(jnp.int32(n // UNIT), n % UNIT)
        if n in plan:
            plan.pop(n)()
    for n in sorted(plan):
        plan[n]()

    grams_part(5, 2, 0, first)
    split_part(5, second)
    rotate_part(5, second)
    rc_go(second)
    grams_part(5, 0, 1, second)
    ry_go((2, 3))
    grams_part(5, 1, 1, second)
    grams_part(5, 2, 1, second)
    p_go((5,))

    for g in range(NG):
        if g == NG - 1:
            for cp in ry.values():
                cp.wait()
            rot[...] = (rots[y] + roty[0] + roty[1] + roty[2]).T
        p_copy(g).wait()
        rows = pl.ds(g * GW, GW)
        gram[rows, :] = pbuf[g, own, :, pl.ds(0, CB)] + precv[g, :, pl.ds(0, CB)]
        stiff[rows, :] = pbuf[g, own, :, pl.ds(CB, CB)] + precv[g, :, pl.ds(CB, CB)]

    pl.when(jnp.logical_not(mine))(send(bt, bt, l_send.at[0], c_recv, other_core).wait_send)
    pl.when(jnp.logical_not(shared_src))(send(bt, bt, l_send.at[1], c_recv, other_core).wait_send)
    last = bt.at[pl.ds(0, GW)]
    pl.when(shared_src)(send(last, last, l_send.at[1], c_recv, other_core).wait_send)
    for cp in sends:
        cp.wait_send()
    c_cp.wait_send()

    drain()


def on_device(basis, image, coeffs):
    dma = pltpu.SemaphoreType.DMA
    return pl.pallas_call(
        kernel,
        out_shape=[
            jax.ShapeDtypeStruct((CB, CB), F32),
            jax.ShapeDtypeStruct((CB, CB), F32),
            jax.ShapeDtypeStruct((RB, OB), F32),
        ],
        in_specs=[pl.BlockSpec(memory_space=pl.ANY)] * 3,
        out_specs=[pl.BlockSpec(memory_space=pltpu.VMEM)] * 3,
        scratch_shapes=[
            pltpu.VMEM((CB, RB), F32),
            pltpu.VMEM((2, NB, CB, RB), F32),
            pltpu.VMEM((2, NB, RB, CB), F32),
            pltpu.VMEM((NB * RB, 2 * CB), BF16),
            pltpu.VMEM((NB * RB, 2 * CB), BF16),
            pltpu.VMEM((2, CB, OB), F32),
            pltpu.VMEM((OB, 2 * CB), BF16),
            pltpu.VMEM((OB, 2 * CB), BF16),
            pltpu.VMEM((4 * GW, NB * RB), BF16),
            pltpu.VMEM((4 * GW, NB * RB), BF16),
            pltpu.VMEM((NG, 2, GW, 2 * CB), F32),
            pltpu.VMEM((NG, GW, 2 * CB), F32),
            pltpu.VMEM((NB, OB, RB), F32),
            pltpu.VMEM((NY, OB, RB), F32),
            pltpu.VMEM((NY, OB, RB), F32),
            pltpu.VMEM((NY - 1, OB, RB), F32),
            dma((NG, 2, NB)),
            dma((2,)),
            dma((2, NG)),
            dma((NG,)),
            dma((2, NB)),
            dma((16,)),
            dma,
            dma((2,)),
            dma((NG,)),
            dma((NG,)),
            dma((NY,)),
            dma((NY,)),
            dma((NY - 1,)),
            dma((NY - 1,)),
        ],
        compiler_params=pltpu.CompilerParams(
            collective_id=0, has_side_effects=True, vmem_limit_bytes=56 * 2**20
        ),
        cost_estimate=pl.CostEstimate(flops=2 * 1610612736 * 3, bytes_accessed=4 * 2**20, transcendentals=0),
    )(basis, image, coeffs)


def solution(mesh):
    return jax.shard_map(
        on_device,
        mesh=mesh,
        in_specs=(P("row", "col"),) * 3,
        out_specs=(P("row", "col"),) * 3,
        check_vma=False,
    )
```

time: 404 us -> 120 us (0.30)
  waiting for transfers between devices: 349 us -> 0 us
  Pallas kernels: 0 us -> 115 us
  matrix products: 30.5 us -> 0 us
  between operations: 13.8 us -> 0.65 us
  other arithmetic: 7.01 us -> 0 us
    all_gather x2 -> x0, waiting for transfers between devices: 192 us -> none  [the longest x1 145 us: on_device(): row_block = lax.all_gather(basis, 'col', axis=1, tiled=True)]
    reduce_scatter x1 -> x0, waiting for transfers between devices: 156 us -> none  [on_device(): lax.psum_scatter(jnp.concatenate([inner_product(columns, basis), inner_pr...]
    pallas_call x0 -> x1, Pallas kernels: none -> 115 us  [on_device(): pl.pallas_call(kernel, out_shape=[jax.ShapeDtypeStruct((CB, CB), F32), ja...]
    dot_general x3 -> x0, matrix products: 30.5 us -> none  [the longest x2 19.9 us: inner_product(): lax.dot_general(left, right, (((0,), (0,)), ((), ())), precision=lax.Prec...]
    concatenate x1 -> x0, other arithmetic: 7.01 us -> none  [on_device(): jnp.concatenate([inner_product(columns, basis), inner_product(columns, im...]
  transfers between devices with their start and end apart: 3 -> 0, of which waited for: 3 -> 0; matrix products, arithmetic and copies ran while one was open for 9% -> 0% of each run, Pallas kernels for 0% -> 0%
where the time goes in v2:
time: 120 us
  Pallas kernels  115 us (96%)
  local copies, waits for them, and re-layouts  3.78 us (3%)
    pallas_call x1, Pallas kernels, on_device(): pl.pallas_call(kernel, out_shape=[jax.ShapeDtypeStruct((CB, CB), F32), ja...  115 us
    unnamed x7, local copies, waits for them, and re-layouts  3.78 us

profile of v2, /device:TPU:1, one launch (start us, length us, event | category | flops | bytes accessed | tf_op | source)
XLA Modules:
  0.0 119.6 jit_solution(9053472387556337761)
XLA Ops:
  0.6 115.2 %shard_map.58 = (f32[384,384]{1,0:T(8,128)}, f32[384,384]{1,0:T(8,128)}, f32[256,256]{1,0:T(8,128)}) custom-call(f32[256,384]{1,0:T(8,128)} %basis.1, f32[256,384]{1,0:T(8,128)} %image.1, f32[384,256]{1,0:T(8,128)} %coeffs.1), custom_call_target="tpu_custom_call" | custom-call | flops 9663676416 | bytes 4194304 | tf_op jit(solution)/shard_map/pallas_call | solution.py:401
  115.9 0.0 copy-start
  115.9 2.0 %copy.9 = f32[384,384]{1,0:T(8,128)} copy(f32[384,384]{1,0:T(8,128)} %get-tuple-element.6) | data formatting | bytes 1179648
  117.8 0.0 copy-done
  117.8 0.0 copy-start.1
  117.8 0.8 copy.10
  118.7 0.3 copy-done.1
  118.9 0.7 copy.11
Async XLA Ops:
  115.9 2.0 %copy-start = (f32[384,384]{1,0:T(8,128)S(1)}, f32[384,384]{1,0:T(8,128)}, u32[]{:S(2)}) copy-start(f32[384,384]{1,0:T(8,128)} %get-tuple-element.7) | copy-start | bytes 1769476
  117.8 1.1 copy-start.1

commit v3 on v2

--- a/solution.py
+++ b/solution.py
@@ -13,12 +13,15 @@
 RB, CB, OB = 256, 384, 256
 NB = 8
 NG, GW = 6, 64
-UNIT = 4
+UNIT = 2
 UNITS = NG * NB // UNIT
-LAG = 1
-END = UNITS + 4 * LAG
-R_NEAR, R_FAR = 7, 9
-SHARED = 2
+LAG, LAG_END = 3, 11
+END = UNITS + LAG_END
+R_NEAR, R_FAR = 14, 19
+RATE = 8
+PIECES = 11
+NS = 4
+SHARED = 0
 
 
 def halves(v):
@@ -86,8 +89,6 @@
     def blk_of(dy, c):
         return lax.rem(y + dy, NY) * 2 + c
 
-    dy_src = lax.rem(y - zs + NY, NY)
-    shared_src = ((dy_src == 1) | (dy_src == 2)) & (core == 0)
     mine = (y == zs) & lead
 
     def gather(g):
@@ -95,11 +96,6 @@
         to = (xh * 8 + zs * 2 + xl, z * 2 + xl)
         pl.when(mine)(pltpu.make_async_copy(src, dst, r).start)
         pl.when(jnp.logical_not(mine))(send(src, dst, l_send.at[0], r, to).start)
-        to = (xh * 8 + zs * 2 + xl, z * 2 + 1 - xl)
-        if g < NG - 1:
-            pl.when(jnp.logical_not(shared_src))(send(src, dst, l_send.at[1], r, to).start)
-        else:
-            send(src, dst, l_send.at[1], r, to).start()
 
     sends = []
 
@@ -129,9 +125,9 @@
         return lbuf.at[slot, blk, pl.ds(pl.multiple_of(g * GW, GW), GW)]
 
     def pass_on(u, k, slot):
-        g, half = lax.div(u, 2), lax.rem(u, 2)
+        g, part = lax.div(u, 4), lax.rem(u, 4)
         c = k % 2
-        blk = blk_of(jnp.where(half == 0, k // 2, 3 - k // 2), c)
+        blk = blk_of(jnp.where(part == 2, 3, jnp.where(part == 3, 2, part)), c)
         src = chunk_ref(g, slot, blk)
 
         def along_z(up):
@@ -148,14 +144,19 @@
             else:
                 pl.when((d > 1) | (d == 1) if c == 1 else d > 1)(lambda: along_z(False))
 
+        shared = (g < NS) & ((part == 1) | (part == 3)) & (k == SHARED)
         if k == SHARED:
-            pl.when(lead | (g == NG - 1))(from_z)
-            pl.when(lead & (g < NG - 1))(send(src, src, x_send.at[g], l_recv.at[g, slot, blk], x_pair).start)
+            pl.when(lead | jnp.logical_not(shared))(from_z)
         else:
             from_z()
+        over = shared | (d == 0) if slot == 0 else shared
+        if slot == 0 or k == SHARED:
+            pl.when(lead & over)(send(src, src, x_send.at[g], l_recv.at[g, slot, blk], x_pair).start)
+
+    lag_b = jnp.where(d == 0, LAG_END, LAG * (4 - d))
 
     def step(t, k):
-        ua, ub = t - LAG * d, t - LAG * (4 - d)
+        ua, ub = t - LAG * d, t - lag_b
         pl.when((ua >= 0) & (ua < UNITS))(lambda: pass_on(ua, k, 0))
         pl.when((ub >= 0) & (ub < UNITS))(lambda: pass_on(ub, k, 1))
 
@@ -169,7 +170,7 @@
 
     def drain():
         for g in range(NG):
-            few = g < NG - 1
+            few = g < NS
             for up in (True, False):
                 s = z_send.at[0 if up else 1, g]
                 part = d == 3 if up else d == 1
@@ -184,8 +185,15 @@
                     pl.when(part & jnp.logical_not(lead))(lambda: sent(2, s))
                 else:
                     pl.when(part)(lambda: sent(4, s))
+            s = x_send.at[g]
             if few:
-                pl.when(lead)(lambda: sent(4, x_send.at[g]))
+                pl.when(lead & (d > 0))(lambda: sent(4, s))
+
+                at = lbuf.at[0, pl.ds(0, 5), pl.ds(0, 2 * GW)]
+                pl.when(lead & (d == 0))(send(at, at, s, l_recv.at[0, 0, 0], other_core).wait_send)
+            else:
+                pl.when(lead & (d == 0))(lambda: sent(8, s))
+
 
     own = jnp.where(lax.div(lax.rem(z - d + NZ, NZ), 4) == xh, 0, 1)
     h_a = jnp.where(own == 0, xh, 1 - xh)
@@ -217,69 +225,44 @@
                 for slot in range(2):
                     arrived(chunk_ref(g, slot, blk), l_recv.at[g, slot, blk])
 
-    def split_l(groups, blks):
-        for b in blks:
-            cols = pl.ds(b * RB, RB)
-            for k, g in enumerate(groups):
-                for slot in range(2):
-                    hi, lo = halves(lbuf[slot, b, pl.ds(g * GW, GW), :])
-                    rows = pl.ds((k * 2 + slot) * GW, GW)
-                    l_hi[rows, cols] = hi
-                    l_lo[rows, cols] = lo
-
-    def grams(groups, n):
-        cols, rows = pl.ds(n * 256, 256), pl.ds(0, len(groups) * 2 * GW)
-        a_hi, b_hi = l_hi[rows, :], r_hi[:, cols]
-        acc = dot(a_hi, b_hi) + dot(l_lo[rows, :], b_hi) + dot(a_hi, r_lo[:, cols])
-        for k, g in enumerate(groups):
-            for slot in range(2):
-                at = (k * 2 + slot) * GW
-                pbuf[g, slot, :, cols] = acc[at : at + GW, :]
-
-    def grams_part(g, n, part, dys):
-        cols, rows, acc = pl.ds(n * 256, 256), pl.ds(0, 2 * GW), 0.0
-        for dy in dys:
-            ks = pl.ds(pl.multiple_of(lax.rem(y + dy, NY) * 2 * RB, 2 * RB), 2 * RB)
-            a_hi, b_hi = l_hi[rows, ks], r_hi[ks, cols]
-            acc += dot(a_hi, b_hi) + dot(l_lo[rows, ks], b_hi) + dot(a_hi, r_lo[ks, cols])
+    def split_l(g, b):
+        cols, at = pl.ds(pl.multiple_of(b * RB, RB), RB), pl.ds(pl.multiple_of(g * GW, GW), GW)
         for slot in range(2):
-            v = acc[slot * GW : slot * GW + GW, :]
-            pbuf[g, slot, :, cols] = v if part == 0 else pbuf[g, slot, :, cols] + v
-
-    def split_part(g, dys):
-        for dy in dys:
+            hi, lo = halves(lbuf[slot, b, at, :])
+            l_hi[pl.ds(slot * GW, GW), cols] = hi
+            l_lo[pl.ds(slot * GW, GW), cols] = lo
+
+    def grams(g, n):
+        cols = pl.ds(pl.multiple_of(n * 256, 256), 256)
+        b_hi = r_hi[:, cols]
+        acc = dot(l_hi[...], b_hi) + dot(l_lo[...], b_hi) + dot(l_hi[...], r_lo[:, cols])
+        for slot in range(2):
+            pbuf[g, slot, :, cols] = acc[slot * GW : slot * GW + GW, :]
+
+    def rotate(g, b):
+        cols, ks = pl.ds(pl.multiple_of(b * RB, RB), RB), pl.ds(pl.multiple_of(g * 2 * GW, 2 * GW), 2 * GW)
+        b_hi, b_lo, a_hi = l_hi[:, cols], l_lo[:, cols], c_hi[:, ks]
+        rotp[b] += dot(a_hi, b_hi) + dot(c_lo[:, ks], b_hi) + dot(a_hi, b_lo)
+
+    def piece(i):
+        g, r = lax.div(i, PIECES), lax.rem(i, PIECES)
+        pl.when((r == 0) & (g < NS))(lambda: shared_arrived(g))
+
+        @pl.when(r < 4)
+        def _():
             for c in range(2):
-                b = blk_of(dy, c)
-                cols = pl.ds(pl.multiple_of(b * RB, RB), RB)
-                for slot in range(2):
-                    hi, lo = halves(lbuf[slot, b, pl.ds(g * GW, GW), :])
-                    l_hi[pl.ds(slot * GW, GW), cols] = hi
-                    l_lo[pl.ds(slot * GW, GW), cols] = lo
-
-    def rotate_part(g, dys):
-        rows, ks = pl.ds(0, 2 * GW), pl.ds(g * 2 * GW, 2 * GW)
-        for dy in dys:
+                split_l(g, r * 2 + c)
+
+        pl.when((r >= 4) & (r < 7))(lambda: grams(g, r - 4))
+        pl.when(r == 6)(lambda: p_copy(g).start())
+
+        @pl.when(r >= 7)
+        def _():
             for c in range(2):
-                b = blk_of(dy, c)
-                cols = pl.ds(pl.multiple_of(b * RB, RB), RB)
-                b_hi, b_lo = l_hi[rows, cols], l_lo[rows, cols]
-                rotp[b] += dot(c_hi[:, ks], b_hi) + dot(c_lo[:, ks], b_hi) + dot(c_hi[:, ks], b_lo)
+                rotate(g, (r - 7) * 2 + c)
 
     def p_copy(g):
         return send(pbuf.at[g, 1 - own], precv.at[g], p_send.at[g], p_recv.at[g], partner)
-
-    def rotate(groups, blks):
-        rows = pl.ds(0, len(groups) * 2 * GW)
-        ks = pl.ds(groups[0] * 2 * GW, len(groups) * 2 * GW)
-        for b in blks:
-            cols = pl.ds(b * RB, RB)
-            b_hi, b_lo = l_hi[rows, cols], l_lo[rows, cols]
-            acc = dot(c_hi[:, ks], b_hi) + dot(c_lo[:, ks], b_hi) + dot(c_hi[:, ks], b_lo)
-            rotp[b] = acc if groups[0] == 0 else rotp[b] + acc
-
-    def p_go(groups):
-        for g in groups:
-            p_copy(g).start()
 
     def r_near():
         for arr in range(2):
@@ -315,65 +298,46 @@
                 ry[dy] = send(rots.at[b], roty.at[dy - 1], ry_send.at[dy - 1], ry_recv.at[dy - 1], dev(dy=dy))
                 ry[dy].start()
 
-    def pair_work(groups):
-        yield lambda: [shared_arrived(g) for g in groups if g < NG - 1] and split_l(groups, range(4))
-        yield lambda: split_l(groups, range(4, 8))
-        yield lambda: grams(groups, 0)
-        yield lambda: grams(groups, 1)
-        yield lambda: grams(groups, 2)
-        yield lambda: p_go(groups)
-        yield lambda: rotate(groups, range(4))
-        yield lambda: rotate(groups, range(4, 8))
-
-    plan = {}
-
-    def at(t, *work):
-        n = t * UNIT
-        for w in work:
-            while n in plan:
-                n += 1
-            plan[n] = w
-
-    at(
-        R_NEAR,
-        r_near,
-        lambda: split_r(blk_of(0, core), False),
-        lambda: split_r(blk_of(0, 1 - core)),
-        lambda: split_r(blk_of(1, core), False),
-        lambda: split_r(blk_of(3, core), False),
-        lambda: split_r(blk_of(1, 1 - core)),
-        lambda: split_r(blk_of(3, 1 - core)),
-        split_c,
-    )
-    at(R_FAR, r_far, lambda: split_r(blk_of(2, core), False), lambda: split_r(blk_of(2, 1 - core)))
-    at(max(R_FAR, 4 + 4 * LAG), *pair_work((0, 1)))
-    at(8 + 4 * LAG, *pair_work((2, 3)))
-    at(10 + 4 * LAG, *pair_work((4,)))
-    first, second = (0, 1), (3, 2)
-    at(
-        11 + 4 * LAG,
-        lambda: split_part(5, first),
-        lambda: rotate_part(5, first),
-        lambda: [rc_go(first), grams_part(5, 0, 0, first)],
-        lambda: [ry_go(first), grams_part(5, 1, 0, first)],
-    )
+    rotp[...] = jnp.zeros_like(rotp)
     loop(0, R_NEAR, unit)
-    for n in range(R_NEAR * UNIT, END * UNIT):
-        step(jnp.int32(n // UNIT), n % UNIT)
-        if n in plan:
-            plan.pop(n)()
-    for n in sorted(plan):
-        plan[n]()
-
-    grams_part(5, 2, 0, first)
-    split_part(5, second)
-    rotate_part(5, second)
-    rc_go(second)
-    grams_part(5, 0, 1, second)
-    ry_go((2, 3))
-    grams_part(5, 1, 1, second)
-    grams_part(5, 2, 1, second)
-    p_go((5,))
+    r_near()
+
+    def with_own(t):
+        unit(t)
+        i = t - R_NEAR
+        split_r(blk_of(jnp.where(i == 2, 3, i), core), False)
+
+    def with_other(t):
+        unit(t)
+        split_r(blk_of(t - (R_NEAR + 3), 1 - core))
+
+    loop(R_NEAR, R_NEAR + 3, with_own)
+    loop(R_NEAR + 3, R_FAR, with_other)
+    r_far()
+    unit(jnp.int32(R_FAR))
+    split_r(blk_of(3, 1 - core))
+    split_c()
+    unit(jnp.int32(R_FAR + 1))
+    split_r(blk_of(2, core), False)
+    split_r(blk_of(2, 1 - core))
+
+    def with_work(t):
+        unit(t)
+        i = t - (R_FAR + 2)
+        most = (NG - 1) * PIECES
+        loop(jnp.minimum(lax.div(i * RATE, 2), most), jnp.minimum(lax.div((i + 1) * RATE, 2), most), piece)
+
+    loop(R_FAR + 2, END, with_work)
+
+    last = NG - 1
+    loop(min((END - R_FAR - 2) * RATE // 2, last * PIECES), last * PIECES, piece)
+    loop(0, NB, lambda b: split_l(last, b))
+    loop(0, NB, lambda b: rotate(last, b))
+    rc_go(range(NY))
+    loop(0, 2, lambda n: grams(last, n))
+    ry_go((2, 1, 3, 0))
+    grams(last, 2)
+    p_copy(last).start()
 
     for g in range(NG):
         if g == NG - 1:
@@ -386,9 +350,6 @@
         stiff[rows, :] = pbuf[g, own, :, pl.ds(CB, CB)] + precv[g, :, pl.ds(CB, CB)]
 
     pl.when(jnp.logical_not(mine))(send(bt, bt, l_send.at[0], c_recv, other_core).wait_send)
-    pl.when(jnp.logical_not(shared_src))(send(bt, bt, l_send.at[1], c_recv, other_core).wait_send)
-    last = bt.at[pl.ds(0, GW)]
-    pl.when(shared_src)(send(last, last, l_send.at[1], c_recv, other_core).wait_send)
     for cp in sends:
         cp.wait_send()
     c_cp.wait_send()
@@ -416,8 +377,8 @@
             pltpu.VMEM((2, CB, OB), F32),
             pltpu.VMEM((OB, 2 * CB), BF16),
             pltpu.VMEM((OB, 2 * CB), BF16),
-            pltpu.VMEM((4 * GW, NB * RB), BF16),
-            pltpu.VMEM((4 * GW, NB * RB), BF16),
+            pltpu.VMEM((2 * GW, NB * RB), BF16),
+            pltpu.VMEM((2 * GW, NB * RB), BF16),
             pltpu.VMEM((NG, 2, GW, 2 * CB), F32),
             pltpu.VMEM((NG, GW, 2 * CB), F32),
             pltpu.VMEM((NB, OB, RB), F32),
@@ -425,7 +386,7 @@
             pltpu.VMEM((NY, OB, RB), F32),
             pltpu.VMEM((NY - 1, OB, RB), F32),
             dma((NG, 2, NB)),
-            dma((2,)),
+            dma((1,)),
             dma((2, NG)),
             dma((NG,)),
             dma((2, NB)),

time: 120 us -> 117 us (0.975)
  Pallas kernels: 115 us -> 112 us
    pallas_call x1, Pallas kernels: 115 us -> 112 us  [on_device(): pl.pallas_call(kernel, out_shape=[jax.ShapeDtypeStruct((CB, CB), F32), ja...]
where the time goes in v3:
time: 117 us
  Pallas kernels  112 us (96%)
  local copies, waits for them, and re-layouts  3.78 us (3%)
    pallas_call x1, Pallas kernels, on_device(): pl.pallas_call(kernel, out_shape=[jax.ShapeDtypeStruct((CB, CB), F32), ja...  112 us
    unnamed x7, local copies, waits for them, and re-layouts  3.78 us

profile of v3, /device:TPU:1, one launch (start us, length us, event | category | flops | bytes accessed | tf_op | source)
XLA Modules:
  0.0 116.5 jit_solution(8908253202021562157)
XLA Ops:
  0.6 112.1 %shard_map.58 = (f32[384,384]{1,0:T(8,128)}, f32[384,384]{1,0:T(8,128)}, f32[256,256]{1,0:T(8,128)}) custom-call(f32[256,384]{1,0:T(8,128)} %basis.1, f32[256,384]{1,0:T(8,128)} %image.1, f32[384,256]{1,0:T(8,128)} %coeffs.1), custom_call_target="tpu_custom_call" | custom-call | flops 9663676416 | bytes 4194304 | tf_op jit(solution)/shard_map/pallas_call | solution.py:362
  112.7 0.0 copy-start
  112.7 2.0 %copy.9 = f32[384,384]{1,0:T(8,128)} copy(f32[384,384]{1,0:T(8,128)} %get-tuple-element.6) | data formatting | bytes 1179648
  114.7 0.0 copy-done
  114.7 0.0 copy-start.1
  114.7 0.8 copy.10
  115.5 0.3 copy-done.1
  115.8 0.7 copy.11
Async XLA Ops:
  112.7 2.0 %copy-start = (f32[384,384]{1,0:T(8,128)S(1)}, f32[384,384]{1,0:T(8,128)}, u32[]{:S(2)}) copy-start(f32[384,384]{1,0:T(8,128)} %get-tuple-element.7) | copy-start | bytes 1769476
  114.7 1.1 copy-start.1
